TPU v7x, 32 devices: a whole 2x2x4 slice. The times are simulated.
32 devices in a mesh: groups: 2 (over y), section: 2 (over core), expert: 8 (over z, x).
Axes of the slice: x: 2, y: 2, z: 4, core: 2. Of those that a mesh axis runs over, the one named last changes fastest.
Arguments:
- hidden_in: bfloat16 [2, 32, 3584], P(None, ('groups', 'expert')), parts along dimension 1, may hold values from -6 to 6
- norm_gain: float32 [2, 3584], P('section'), may hold values from 0.1 to 1.9
- gate_weight: bfloat16 [2, 3584, 1024], P('section', None, 'expert'), may hold values from -0.09375 to 0.09375
- up_weight: bfloat16 [2, 3584, 1024], P('section', None, 'expert'), may hold values from -0.09375 to 0.09375
- down_weight: bfloat16 [2, 1024, 3584], P('section', 'expert'), may hold values from -0.5 to 0.5
- routes: int32 [2, 2, 32, 4], P('section', None, ('groups', 'expert')), parts along dimension 2, may hold values from 0 to 7, all different within a row; in each aligned block of 2 rows (0 to 1, 2 to 3, ..., all dimensions but the last counted through in order) at most 2 rows name the same one
- route_weights: float32 [2, 2, 32, 4], P('section', None, ('groups', 'expert')), parts along dimension 2, may hold values from 0.2 to 1
- queries: bfloat16 [2, 2, 32, 64, 576], P('section', None, ('groups', 'expert')), parts along dimension 2, may hold values from -18 to 18
- latent_cache: bfloat16 [2, 2, 32, 64, 576], P('section', None, ('groups', 'expert')), parts along dimension 2, may hold values from -4.5 to 4.5
- lengths: int32 [2, 32], P(None, ('groups', 'expert')), parts along dimension 1, may hold values from 16 to 64, as said below
Outputs:
- layer_out: bfloat16 [2, 2, 32, 3584], P('section', None, ('groups', 'expert')), parts along dimension 2
- attention_out: bfloat16 [2, 2, 32, 64, 512], P('section', None, ('groups', 'expert')), parts along dimension 2
There are 2 independent parts, one for each index of `groups`. A program takes and returns all parts, laid end to end along the dimension named above; an argument that names none is the same for every part. Nothing has to cross between parts.
Inputs may be any that keep to these rules, and one draw needn't show every extreme that they name: `routes`: each row names 4 different experts; in every aligned block of 2 rows of one layer and micro-batch no expert is named by more than 2 rows, and in some blocks some expert is named by exactly 2. `lengths`: in every block of 2 rows the first row has length 64.
All inputs are finite; a program needn't handle non-finite values.
Results may differ from a plain program's by a relative error of at most 0.007.
Values may be sent and summed in bfloat16 or wider, within the bound.
A program may use at most 64 MiB of HBM per device.

v0:
```python
import jax
import jax.numpy as jnp
from jax import lax
from jax.sharding import PartitionSpec as P

EXPERTS = 8
LAT = 512
CAP = 2


att_scale = 0.07216878364870322


def from_behind(value, axis, steps):
    count = lax.axis_size(axis)
    first, last = (max(0, -steps), min(count, count - steps))
    return lax.ppermute(value, axis, [(source, source + steps) for source in range(first, last)])


def rms_normed(wide_input, norm_scale):
    mean_square = jnp.mean(wide_input * wide_input, axis=-1, keepdims=True)
    return (wide_input * lax.rsqrt(mean_square + 1e-06) * norm_scale).astype(jnp.bfloat16)


def pair_slots(route_blocks):
    onehot = (route_blocks[..., None] == jnp.arange(EXPERTS, dtype=jnp.int32)).astype(jnp.int32)
    earlier = jnp.cumsum(onehot, axis=1) - onehot
    return jnp.sum(earlier * onehot, axis=-1)


def expert_rows(received, w_gate, w_up, w_down):
    flat_rows = received.reshape(-1, received.shape[-1])
    gate_proj = jnp.dot(flat_rows, w_gate, preferred_element_type=jnp.float32)
    up_proj = jnp.dot(flat_rows, w_up, preferred_element_type=jnp.float32)
    activation = (jax.nn.silu(gate_proj) * up_proj).astype(jnp.bfloat16)
    partial_terms = jnp.dot(activation, w_down, preferred_element_type=jnp.float32).astype(
        jnp.bfloat16
    )
    return partial_terms.reshape(received.shape)


def moe_step(hidden, norm_scale, w_gate, w_up, w_down, route_now, weight_now):
    row_count, model_width = hidden.shape
    top_count = route_now.shape[1]
    devices = lax.axis_size("expert")
    group_size = devices // EXPERTS
    wide_input = hidden.astype(jnp.float32)
    normed = rms_normed(wide_input, norm_scale)
    pair_routes = route_now.reshape(row_count * top_count)
    slot_index = pair_slots(pair_routes[None, :])[0]
    placement = (
        pair_routes[:, None, None] == jnp.arange(EXPERTS, dtype=jnp.int32)[None, :, None]
    ) & (slot_index[:, None, None] == jnp.arange(CAP, dtype=jnp.int32)[None, None, :])
    placement = jnp.sum(
        placement.reshape(row_count, top_count, EXPERTS * CAP).astype(jnp.int32), axis=1
    ).astype(jnp.bfloat16)
    per_expert = jnp.einsum(
        "rs,rd->sd", placement, normed, preferred_element_type=jnp.float32
    ).astype(jnp.bfloat16)
    outgoing = jnp.broadcast_to(
        per_expert.reshape(EXPERTS, 1, CAP, model_width), (EXPERTS, group_size, CAP, model_width)
    ).reshape(devices, CAP, model_width)
    partial_out = expert_rows(
        lax.all_to_all(outgoing, "expert", split_axis=0, concat_axis=0, tiled=True),
        w_gate,
        w_up,
        w_down,
    )
    returned = lax.all_to_all(partial_out, "expert", split_axis=0, concat_axis=0, tiled=True)
    summed = jnp.sum(
        returned.reshape(EXPERTS, group_size, CAP, model_width).astype(jnp.float32), axis=1
    )
    summed = summed.reshape(EXPERTS * CAP, model_width)
    picked = jnp.take(summed, pair_routes * CAP + slot_index, axis=0).reshape(
        row_count, top_count, model_width
    )
    combined = jnp.sum(weight_now[..., None] * picked, axis=1)
    return (wide_input + combined).astype(jnp.bfloat16)


def attend(query_rows, cache_rows, length_rows):
    scores = (
        jnp.einsum("rhc,rlc->rhl", query_rows, cache_rows, preferred_element_type=jnp.float32)
        * att_scale
    )
    visible = (
        jnp.arange(cache_rows.shape[1], dtype=jnp.int32)[None, None, :] < length_rows[:, None, None]
    )
    scores = jnp.where(visible, scores, -jnp.inf)
    row_maximum = jnp.max(scores, axis=-1, keepdims=True)
    expanded = jnp.exp(scores - row_maximum)
    probabilities = (expanded / jnp.sum(expanded, axis=-1, keepdims=True)).astype(jnp.bfloat16)
    return jnp.einsum(
        "rhl,rlc->rhc", probabilities, cache_rows[..., :LAT], preferred_element_type=jnp.float32
    ).astype(jnp.bfloat16)


def shards(
    hidden_in,
    norm_gain,
    gate_weight,
    up_weight,
    down_weight,
    routes,
    route_weights,
    queries,
    latent_cache,
    lengths,
):
    section_index = lax.axis_index("section")
    micro_count = hidden_in.shape[0]
    incoming = jnp.zeros(hidden_in.shape[1:], jnp.bfloat16)
    layer_results = []
    attention_results = []
    for step_index in range(micro_count + 1):
        first_input = hidden_in[min(step_index, micro_count - 1)]
        layer_input = jnp.where(section_index == 0, first_input, incoming)
        batch_index = jnp.clip(step_index - section_index, 0, micro_count - 1)
        route_now = lax.dynamic_index_in_dim(routes[0], batch_index, 0, keepdims=False)
        weight_now = lax.dynamic_index_in_dim(route_weights[0], batch_index, 0, keepdims=False)
        result = moe_step(
            layer_input,
            norm_gain[0],
            gate_weight[0],
            up_weight[0],
            down_weight[0],
            route_now,
            weight_now,
        )
        layer_results.append(result)
        if step_index < micro_count:
            incoming = from_behind(result, "section", 1)
            attention_results.append(
                attend(queries[0, step_index], latent_cache[0, step_index], lengths[step_index])
            )
    layer_out = jnp.stack(
        [
            jnp.where(section_index == 0, layer_results[batch], layer_results[batch + 1])
            for batch in range(micro_count)
        ]
    )[None]
    attention_out = jnp.stack(attention_results)[None]
    return (layer_out, attention_out)


def solution(mesh):
    return jax.shard_map(
        shards,
        mesh=mesh,
        in_specs=(
            P(None, ("groups", "expert"), None),
            P("section", None),
            P("section", None, "expert"),
            P("section", None, "expert"),
            P("section", "expert", None),
            P("section", None, ("groups", "expert"), None),
            P("section", None, ("groups", "expert"), None),
            P("section", None, ("groups", "expert"), None, None),
            P("section", None, ("groups", "expert"), None, None),
            P(None, ("groups", "expert")),
        ),
        out_specs=(
            P("section", None, ("groups", "expert"), None),
            P("section", None, ("groups", "expert"), None, None),
        ),
        check_vma=False,
    )
```

profile of v0, /device:TPU:0, one launch (start us, length us, event | category | flops | bytes accessed | tf_op | source)
XLA Modules:
  0.0 86.8 jit_solution(667523257888631093)
XLA Ops:
  0.7 0.7 copy-done.7
  1.9 0.3 reduce_sum.139
  2.3 0.3 copy-done.5
  2.7 0.6 copy-done.6
  3.3 0.2 convolution_convert_fusion.5
  3.5 0.7 reshape_reshape.9
  4.2 7.3 %all-to-all-start = ((bf16[8,2,3584]{2,1,0:T(2,128)(2,1)}), bf16[8,2,3584]{2,1,0:T(2,128)(2,1)S(1)}, u32[]{:S(2)}, u32[]{:S(2)}) async-start(bf16[8,2,3584]{2,1,0:T(2,128)(2,1)} %reshape_reshape.9), calls=%async_computation | async-start | bytes 229376 | tf_op jit(solution)/shard_map/all_to_all | solution.py:64
  11.7 0.7 copy-done.8
  12.9 0.5 copy-done.9
  13.6 0.8 copy-done.10
  14.4 0.2 fusion.9
  14.7 0.2 fusion.8
  15.0 0.9 %fusion.2 = bf16[1,2,64,512]{3,2,1,0:T(8,128)(2,1)} fusion(bf16[2,64,576]{2,1,0:T(8,128)(2,1)S(1)} %get-tuple-element.15, f32[2,64]{1,0:T(2,128)S(1)} %fusion.90, f32[2,64,64]{1,2,0:T(8,128)S(1)} %fusion.9), kind=kOutput, calls=%fused_computation.13 | convolution fusion | flops 8478911 | bytes 394240 | tf_op jit(solution)/shard_map/rhl,rlc->rhc/dot_general | solution.py:93
  15.9 2.9 %all-to-all-done = bf16[8,2,3584]{2,1,0:T(2,128)(2,1)S(1)} async-done(((bf16[8,2,3584]{2,1,0:T(2,128)(2,1)}), bf16[8,2,3584]{2,1,0:T(2,128)(2,1)S(1)}, u32[]{:S(2)}, u32[]{:S(2)}) %all-to-all-start) | async-done | bytes 114720 | tf_op jit(solution)/shard_map/all_to_all | solution.py:64
  18.8 0.2 fusion.26
  19.0 0.4 convolution_convert_fusion.4
  19.5 0.7 reshape.625
  20.2 3.4 %all-to-all-start.1 = ((bf16[8,2,3584]{2,1,0:T(2,128)(2,1)}), bf16[8,2,3584]{2,1,0:T(2,128)(2,1)S(1)}, u32[]{:S(2)}, u32[]{:S(2)}) async-start(bf16[8,2,3584]{2,1,0:T(2,128)(2,1)} %reshape.625), calls=%async_computation.1 | async-start | bytes 229376 | tf_op jit(solution)/shard_map/all_to_all | solution.py:69
  23.6 7.2 %all-to-all-done.1 = bf16[8,2,3584]{2,1,0:T(2,128)(2,1)S(1)} async-done(((bf16[8,2,3584]{2,1,0:T(2,128)(2,1)}), bf16[8,2,3584]{2,1,0:T(2,128)(2,1)S(1)}, u32[]{:S(2)}, u32[]{:S(2)}) %all-to-all-start.1) | async-done | bytes 114720 | tf_op jit(solution)/shard_map/all_to_all | solution.py:69
  30.8 0.6 gather_fusion
  31.6 1.3 %collective-permute-start = (bf16[2,3584]{1,0:T(2,128)(2,1)S(1)}, bf16[2,3584]{1,0:T(2,128)(2,1)S(1)}, u32[]{:S(2)}, u32[]{:S(2)}) collective-permute-start(bf16[2,3584]{1,0:T(2,128)(2,1)S(1)} %fusion.47), channel_id=1, source_target_pairs={{0,8},{1,9},{2,10},{3,11},{4,12},{5,13},{6,14},{7,15},{16,24},{17,... | collective-permute-start | bytes 43016 | tf_op jit(solution)/shard_map/ppermute | solution.py:17
  33.1 0.3 reduce_sum.143
  33.4 0.4 collective-permute-done
  33.9 0.2 convolution_convert_fusion.3
  34.2 0.7 reshape_reshape.10
  34.8 3.4 %all-to-all-start.2 = ((bf16[8,2,3584]{2,1,0:T(2,128)(2,1)}), bf16[8,2,3584]{2,1,0:T(2,128)(2,1)S(1)}, u32[]{:S(2)}, u32[]{:S(2)}) async-start(bf16[8,2,3584]{2,1,0:T(2,128)(2,1)} %reshape_reshape.10), calls=%async_computation.2 | async-start | bytes 229376 | tf_op jit(solution)/shard_map/all_to_all | solution.py:64
  38.2 7.5 %all-to-all-done.2 = bf16[8,2,3584]{2,1,0:T(2,128)(2,1)S(1)} async-done(((bf16[8,2,3584]{2,1,0:T(2,128)(2,1)}), bf16[8,2,3584]{2,1,0:T(2,128)(2,1)S(1)}, u32[]{:S(2)}, u32[]{:S(2)}) %all-to-all-start.2) | async-done | bytes 114720 | tf_op jit(solution)/shard_map/all_to_all | solution.py:64
  45.7 0.2 fusion.24
  46.0 0.4 convolution_convert_fusion.2
  46.4 0.7 reshape.630
  47.1 3.4 %all-to-all-start.3 = ((bf16[8,2,3584]{2,1,0:T(2,128)(2,1)}), bf16[8,2,3584]{2,1,0:T(2,128)(2,1)S(1)}, u32[]{:S(2)}, u32[]{:S(2)}) async-start(bf16[8,2,3584]{2,1,0:T(2,128)(2,1)} %reshape.630), calls=%async_computation.3 | async-start | bytes 229376 | tf_op jit(solution)/shard_map/all_to_all | solution.py:69
  50.5 7.2 %all-to-all-done.3 = bf16[8,2,3584]{2,1,0:T(2,128)(2,1)S(1)} async-done(((bf16[8,2,3584]{2,1,0:T(2,128)(2,1)}), bf16[8,2,3584]{2,1,0:T(2,128)(2,1)S(1)}, u32[]{:S(2)}, u32[]{:S(2)}) %all-to-all-start.3) | async-done | bytes 114720 | tf_op jit(solution)/shard_map/all_to_all | solution.py:69
  57.7 0.6 gather_fusion.1
  58.6 1.3 %collective-permute-start.1 = (bf16[2,3584]{1,0:T(2,128)(2,1)S(1)}, bf16[2,3584]{1,0:T(2,128)(2,1)S(1)}, u32[]{:S(2)}, u32[]{:S(2)}) collective-permute-start(bf16[2,3584]{1,0:T(2,128)(2,1)S(1)} %get-tuple-element.4), channel_id=1, source_target_pairs={{0,8},{1,9},{2,10},{3,11},{4,12},{5,13},{6,14},{7,15},{16,24},{17,... | collective-permute-start | bytes 43016 | tf_op jit(solution)/shard_map/ppermute | solution.py:17
  59.9 1.2 %fusion.3 = bf16[1,2,64,512]{3,2,1,0:T(8,128)(2,1)S(1)} fusion(bf16[2,64,576]{2,1,0:T(8,128)(2,1)S(1)} %get-tuple-element.16, f32[2,64]{1,0:T(2,128)S(1)} %fusion.89, f32[2,64,64]{1,2,0:T(8,128)} %copy-done.11), kind=kOutput, calls=%fused_computation.14 | convolution fusion | flops 8478911 | bytes 394240 | tf_op jit(solution)/shard_map/rhl,rlc->rhc/dot_general | solution.py:93
  61.2 0.3 reduce_sum.147
  61.7 0.2 convolution_convert_fusion.1
  61.9 0.7 reshape_reshape.11
  62.6 3.4 %all-to-all-start.4 = ((bf16[8,2,3584]{2,1,0:T(2,128)(2,1)}), bf16[8,2,3584]{2,1,0:T(2,128)(2,1)S(1)}, u32[]{:S(2)}, u32[]{:S(2)}) async-start(bf16[8,2,3584]{2,1,0:T(2,128)(2,1)} %reshape_reshape.11), calls=%async_computation.4 | async-start | bytes 229376 | tf_op jit(solution)/shard_map/all_to_all | solution.py:64
  66.0 7.2 %all-to-all-done.4 = bf16[8,2,3584]{2,1,0:T(2,128)(2,1)S(1)} async-done(((bf16[8,2,3584]{2,1,0:T(2,128)(2,1)}), bf16[8,2,3584]{2,1,0:T(2,128)(2,1)S(1)}, u32[]{:S(2)}, u32[]{:S(2)}) %all-to-all-start.4) | async-done | bytes 114720 | tf_op jit(solution)/shard_map/all_to_all | solution.py:64
  73.2 0.2 fusion.22
  73.4 0.4 convolution_convert_fusion
  73.9 0.7 reshape.635
  74.6 3.5 %all-to-all-start.5 = ((bf16[8,2,3584]{2,1,0:T(2,128)(2,1)}), bf16[8,2,3584]{2,1,0:T(2,128)(2,1)S(1)}, u32[]{:S(2)}, u32[]{:S(2)}) async-start(bf16[8,2,3584]{2,1,0:T(2,128)(2,1)} %reshape.635), calls=%async_computation.5 | async-start | bytes 229376 | tf_op jit(solution)/shard_map/all_to_all | solution.py:69
  78.1 0.7 maximum_bitcast_fusion
  78.8 6.4 %all-to-all-done.5 = bf16[8,2,3584]{2,1,0:T(2,128)(2,1)S(1)} async-done(((bf16[8,2,3584]{2,1,0:T(2,128)(2,1)}), bf16[8,2,3584]{2,1,0:T(2,128)(2,1)S(1)}, u32[]{:S(2)}, u32[]{:S(2)}) %all-to-all-start.5) | async-done | bytes 114720 | tf_op jit(solution)/shard_map/all_to_all | solution.py:69
  85.3 0.6 gather_fusion.2
  86.2 0.7 maximum_bitcast_fusion.1
  (81 shorter events, 3.3 us)
Async XLA Ops:
  0.6 18.4 %copy-start = (bf16[1,128,3584]{2,1,0:T(8,128)(2,1)S(1)}, bf16[1,128,3584]{2,1,0:T(8,128)(2,1)}, u32[]{:S(2)}) copy-start(bf16[1,128,3584]{2,1,0:T(8,128)(2,1)} %param.16) | copy-start | bytes 2752516
  0.7 0.8 copy-start.7
  1.8 0.8 copy-start.5
  2.6 0.7 copy-start.6
  3.3 10.1 %copy-start.3 = (bf16[1,2,2,64,576]{4,3,2,1,0:T(8,128)(2,1)S(1)}, bf16[1,2,2,64,576]{4,3,2,1,0:T(8,128)(2,1)}, u32[]{:S(2)}) copy-start(bf16[1,2,2,64,576]{4,3,2,1,0:T(8,128)(2,1)} %param.20) | copy-start | bytes 884740
  4.2 14.5 %all-to-all-start = ((bf16[8,2,3584]{2,1,0:T(2,128)(2,1)}), bf16[8,2,3584]{2,1,0:T(2,128)(2,1)S(1)}, u32[]{:S(2)}, u32[]{:S(2)}) async-start(bf16[8,2,3584]{2,1,0:T(2,128)(2,1)} %reshape_reshape.9), calls=%async_computation | async-start | bytes 229376 | tf_op jit(solution)/shard_map/all_to_all | solution.py:64
  11.7 0.7 copy-start.8
  12.7 0.7 copy-start.9
  13.4 1.0 %copy-start.10 = (bf16[1,2,2,64,576]{4,3,2,1,0:T(8,128)(2,1)S(1)}, bf16[1,2,2,64,576]{4,3,2,1,0:T(8,128)(2,1)}, u32[]{:S(2)}) copy-start(bf16[1,2,2,64,576]{4,3,2,1,0:T(8,128)(2,1)} %param.19) | copy-start | bytes 884740
  13.5 5.3 %copy-start.1 = (bf16[1,3584,128]{2,1,0:T(8,128)(2,1)S(1)}, bf16[1,3584,128]{2,1,0:T(8,128)(2,1)}, u32[]{:S(2)}) copy-start(bf16[1,3584,128]{2,1,0:T(8,128)(2,1)} %param.14) | copy-start | bytes 2752516
  14.9 1.0 %copy-start.11 = (f32[2,64,64]{1,2,0:T(8,128)}, f32[2,64,64]{1,2,0:T(8,128)S(1)}, u32[]{:S(2)}) copy-start(f32[2,64,64]{1,2,0:T(8,128)S(1)} %fusion.8) | copy-start | bytes 98308
  14.9 4.1 %copy-start.2 = (bf16[1,3584,128]{2,1,0:T(8,128)(2,1)S(1)}, bf16[1,3584,128]{2,1,0:T(8,128)(2,1)}, u32[]{:S(2)}) copy-start(bf16[1,3584,128]{2,1,0:T(8,128)(2,1)} %param.15) | copy-start | bytes 2752516
  20.2 10.5 %all-to-all-start.1 = ((bf16[8,2,3584]{2,1,0:T(2,128)(2,1)}), bf16[8,2,3584]{2,1,0:T(2,128)(2,1)S(1)}, u32[]{:S(2)}, u32[]{:S(2)}) async-start(bf16[8,2,3584]{2,1,0:T(2,128)(2,1)} %reshape.625), calls=%async_computation.1 | async-start | bytes 229376 | tf_op jit(solution)/shard_map/all_to_all | solution.py:69
  31.6 2.1 %collective-permute-start = (bf16[2,3584]{1,0:T(2,128)(2,1)S(1)}, bf16[2,3584]{1,0:T(2,128)(2,1)S(1)}, u32[]{:S(2)}, u32[]{:S(2)}) collective-permute-start(bf16[2,3584]{1,0:T(2,128)(2,1)S(1)} %fusion.47), channel_id=1, source_target_pairs={{0,8},{1,9},{2,10},{3,11},{4,12},{5,13},{6,14},{7,15},{16,24},{17,... | collective-permute-start | bytes 43016 | tf_op jit(solution)/shard_map/ppermute | solution.py:17
  34.8 10.8 %all-to-all-start.2 = ((bf16[8,2,3584]{2,1,0:T(2,128)(2,1)}), bf16[8,2,3584]{2,1,0:T(2,128)(2,1)S(1)}, u32[]{:S(2)}, u32[]{:S(2)}) async-start(bf16[8,2,3584]{2,1,0:T(2,128)(2,1)} %reshape_reshape.10), calls=%async_computation.2 | async-start | bytes 229376 | tf_op jit(solution)/shard_map/all_to_all | solution.py:64
  47.1 10.5 %all-to-all-start.3 = ((bf16[8,2,3584]{2,1,0:T(2,128)(2,1)}), bf16[8,2,3584]{2,1,0:T(2,128)(2,1)S(1)}, u32[]{:S(2)}, u32[]{:S(2)}) async-start(bf16[8,2,3584]{2,1,0:T(2,128)(2,1)} %reshape.630), calls=%async_computation.3 | async-start | bytes 229376 | tf_op jit(solution)/shard_map/all_to_all | solution.py:69
  58.6 2.9 %collective-permute-start.1 = (bf16[2,3584]{1,0:T(2,128)(2,1)S(1)}, bf16[2,3584]{1,0:T(2,128)(2,1)S(1)}, u32[]{:S(2)}, u32[]{:S(2)}) collective-permute-start(bf16[2,3584]{1,0:T(2,128)(2,1)S(1)} %get-tuple-element.4), channel_id=1, source_target_pairs={{0,8},{1,9},{2,10},{3,11},{4,12},{5,13},{6,14},{7,15},{16,24},{17,... | collective-permute-start | bytes 43016 | tf_op jit(solution)/shard_map/ppermute | solution.py:17
  62.6 10.5 %all-to-all-start.4 = ((bf16[8,2,3584]{2,1,0:T(2,128)(2,1)}), bf16[8,2,3584]{2,1,0:T(2,128)(2,1)S(1)}, u32[]{:S(2)}, u32[]{:S(2)}) async-start(bf16[8,2,3584]{2,1,0:T(2,128)(2,1)} %reshape_reshape.11), calls=%async_computation.4 | async-start | bytes 229376 | tf_op jit(solution)/shard_map/all_to_all | solution.py:64
  74.6 3.5 %copy-start.4 = (bf16[1,2,64,512]{3,2,1,0:T(8,128)(2,1)S(1)}, bf16[1,2,64,512]{3,2,1,0:T(8,128)(2,1)}, u32[]{:S(2)}) copy-start(bf16[1,2,64,512]{3,2,1,0:T(8,128)(2,1)} %fusion.2) | copy-start | bytes 393220
  74.6 10.7 %all-to-all-start.5 = ((bf16[8,2,3584]{2,1,0:T(2,128)(2,1)}), bf16[8,2,3584]{2,1,0:T(2,128)(2,1)S(1)}, u32[]{:S(2)}, u32[]{:S(2)}) async-start(bf16[8,2,3584]{2,1,0:T(2,128)(2,1)} %reshape.635), calls=%async_computation.5 | async-start | bytes 229376 | tf_op jit(solution)/shard_map/all_to_all | solution.py:69
where the time goes:
time: 87.8 us; the launch traced here: 86.8 us
  waiting for transfers between devices  38.6 us (44%)
  starting transfers between devices  26.8 us (31%)
  local copies, waits for them, and re-layouts  10.5 us (12%)
  matrix products  5.14 us (6%)
  other arithmetic  4.79 us (5%)
  between operations  1.03 us (1%)
    all_to_all x3, waiting for transfers between devices, moe_step(): lax.all_to_all(partial_out, 'expert', split_axis=0, concat_axis=0, tiled=...  20.7 us
    all_to_all x3, waiting for transfers between devices, moe_step(): lax.all_to_all(outgoing, 'expert', split_axis=0, concat_axis=0, tiled=True)  17.5 us
    all_to_all x3, starting transfers between devices, moe_step(): lax.all_to_all(outgoing, 'expert', split_axis=0, concat_axis=0, tiled=True)  14 us
    all_to_all x3, starting transfers between devices, moe_step(): lax.all_to_all(partial_out, 'expert', split_axis=0, concat_axis=0, tiled=...  10.2 us
    unnamed x24, local copies, waits for them, and re-layouts  3.66 us
    ppermute x2, starting transfers between devices, from_behind(): lax.ppermute(value, axis, [(source, source + steps) for source in range(f...  2.58 us
    reshape x3, local copies, waits for them, and re-layouts, expert_rows(): return partial_terms.reshape(received.shape)  2.13 us
    dot_general x2, matrix products, attend(): jnp.einsum('rhl,rlc->rhc', probabilities, cache_rows[..., :LAT], preferre...  2.06 us
  transfers between devices with their start and end apart: 8, of which 7 were waited for; matrix products, arithmetic and copies ran while one was open for 6% of the time, Pallas kernels for 0%

commit v1 on v0

v1 whole, which is shorter than its diff:
```python
import functools

import jax
import jax.numpy as jnp
from jax import lax
from jax.experimental import pallas as pl
from jax.experimental.pallas import tpu as pltpu
from jax.sharding import PartitionSpec as P

EXPERTS = 8
LAT = 512
FOLD = 4

att_scale = 0.07216878364870322


def loop(count, body):
    if count <= 8:
        for step in range(count):
            body(step)
    else:

        @pl.loop(0, count)
        def _(step):
            body(step)


def kernel(
    n,
    hid,
    gain,
    wg,
    wu,
    wd,
    routes,
    rweights,
    queries,
    cache,
    lens,
    lo,
    ao,
    xs,
    g16,
    rt16,
    rw16,
    tab,
    tab_in,
    sbuf,
    disp,
    pout,
    ret,
    xb,
    xb_in,
    wgu_v,
    wd_v,
    q_v,
    c_v,
    ao_v,
    load_sem,
    out_sem,
    d_send,
    d_recv,
    r_send,
    r_recv,
    t_send,
    t_recv,
    x_send,
    x_recv,
):
    sec = lax.axis_index("section")
    me = lax.axis_index("expert")
    micro, rows, width = hid.shape
    fold = width // FOLD
    per = micro * rows
    tall = FOLD * per
    hidden_units = wg.shape[2]
    group = n // EXPERTS

    loads = [
        pltpu.make_async_copy(wg.at[0], wgu_v.at[:, pl.ds(0, hidden_units)], load_sem.at[0]),
        pltpu.make_async_copy(
            wu.at[0], wgu_v.at[:, pl.ds(hidden_units, hidden_units)], load_sem.at[1]
        ),
        pltpu.make_async_copy(wd.at[0], wd_v, load_sem.at[2]),
        pltpu.make_async_copy(queries.at[0], q_v, load_sem.at[3]),
        pltpu.make_async_copy(cache.at[0], c_v, load_sem.at[4]),
    ]
    for copy in loads:
        copy.start()

    barrier = pltpu.get_barrier_semaphore()

    def greet(step):
        other = lax.rem(me + step + 1, n)
        pl.semaphore_signal(
            barrier, inc=1, device_id={"expert": other}, device_id_type=pl.DeviceIdType.MESH
        )

    def greet_across(step):
        other = lax.rem(me + step, n)
        pl.semaphore_signal(
            barrier,
            inc=1,
            device_id={"section": 1 - sec, "expert": other},
            device_id_type=pl.DeviceIdType.MESH,
        )

    loop(n - 1, greet)
    loop(n, greet_across)

    for q in range(FOLD):
        columns = pl.ds(q * fold, fold)
        g16[pl.ds(q * per, per), :] = jnp.broadcast_to(gain[:, columns], (per, fold))
        for m in range(micro):
            at = pl.ds(q * per + m * rows, rows)
            xs[at, :] = hid[m, :, columns].astype(jnp.float32)
            rt16[at, :] = routes[0, m]
            rw16[at, :] = rweights[0, m]
    chosen = rt16[...]
    chosen_weight = rw16[...]
    lanes = lax.broadcasted_iota(jnp.int32, (tall, 128), 1)
    table = jnp.zeros((tall, 128), jnp.float32)
    for k in range(chosen.shape[1]):
        table += jnp.where(chosen[:, k : k + 1] == lanes, chosen_weight[:, k : k + 1], 0.0)
    tab[...] = table

    def table_copy():
        return pltpu.make_async_remote_copy(
            src_ref=tab,
            dst_ref=tab_in,
            send_sem=t_send,
            recv_sem=t_recv,
            device_id={"section": 1},
            device_id_type=pl.DeviceIdType.MESH,
        )

    def back_copy():
        return pltpu.make_async_remote_copy(
            src_ref=xb,
            dst_ref=xb_in,
            send_sem=x_send,
            recv_sem=x_recv,
            device_id={"section": 0},
            device_id_type=pl.DeviceIdType.MESH,
        )

    def dispatch_copy(slot, other):
        return pltpu.make_async_remote_copy(
            src_ref=sbuf,
            dst_ref=disp.at[slot],
            send_sem=d_send.at[other],
            recv_sem=d_recv.at[slot],
            device_id={"expert": other},
            device_id_type=pl.DeviceIdType.MESH,
        )

    def return_copy(phase, slot, other):
        return pltpu.make_async_remote_copy(
            src_ref=pout.at[other],
            dst_ref=ret.at[phase, slot],
            send_sem=r_send.at[other],
            recv_sem=r_recv.at[phase, slot],
            device_id={"section": 1, "expert": other},
            device_id_type=pl.DeviceIdType.MESH,
        )

    def attend():
        loads[3].wait()
        loads[4].wait()
        positions = lax.broadcasted_iota(jnp.int32, (queries.shape[3], cache.shape[3]), 1)
        for m in range(micro):
            for r in range(rows):
                entries = c_v[m, r]
                scores = (
                    lax.dot_general(
                        q_v[m, r],
                        entries,
                        (((1,), (1,)), ((), ())),
                        preferred_element_type=jnp.float32,
                    )
                    * att_scale
                )
                scores = jnp.where(positions < lens[m, r], scores, -jnp.inf)
                expanded = jnp.exp(scores - jnp.max(scores, axis=1, keepdims=True))
                probs = (expanded / jnp.sum(expanded, axis=1, keepdims=True)).astype(jnp.bfloat16)
                ao_v[m, r] = jnp.dot(
                    probs, entries[:, :LAT], preferred_element_type=jnp.float32
                ).astype(jnp.bfloat16)
        pltpu.make_async_copy(ao_v, ao.at[0], out_sem).start()

    def combine(phase, weights, skip_own):
        total = xs[...]
        for e in range(EXPERTS):
            weight = weights[:, e : e + 1]

            def one(g, total):
                slot = e * group + g
                if skip_own:

                    @pl.when(slot != me)
                    def _():
                        return_copy(phase, slot, slot).wait_recv()

                else:
                    return_copy(phase, slot, slot).wait_recv()
                return total + weight * ret[phase, slot].astype(jnp.float32)

            if group == 1:
                total = one(0, total)
            else:
                total = lax.fori_loop(0, group, one, total)
        return total.astype(jnp.bfloat16)

    def emit(values):
        xs[...] = values.astype(jnp.float32)
        for q in range(FOLD):
            for m in range(micro):
                lo[0, m, :, pl.ds(q * fold, fold)] = xs[
                    pl.ds(q * per + m * rows, rows), :
                ].astype(jnp.bfloat16)

    pl.semaphore_wait(barrier, 2 * n - 1)

    @pl.when(sec == 0)
    def _():
        table_copy().start()

    @pl.when(sec == 1)
    def _():
        attend()
        table_copy().wait_recv()
        first = combine(0, tab_in[...], False)
        xb[...] = first
        back_copy().start()
        xs[...] = first.astype(jnp.float32)

    wide = xs[...]
    squares = jnp.sum(wide * wide, axis=1, keepdims=True)
    halves = jnp.broadcast_to(squares[: tall // 2] + squares[tall // 2 :], (tall // 2, 128))
    halves = halves + pltpu.roll(halves, per, 0)
    scale = lax.rsqrt(halves[:, :1] / width + 1e-06)
    scale = jnp.concatenate([scale, scale], axis=0)
    normed = (wide * scale * g16[...]).astype(jnp.bfloat16)
    sbuf[...] = normed
    disp[me] = normed

    def send(step):
        dispatch_copy(me, lax.rem(me + step + 1, n)).start()

    loop(n - 1, send)
    for copy in loads[:3]:
        copy.wait()

    chunk = 8
    flat = chunk * tall
    low_row = lax.broadcasted_iota(jnp.int32, (chunk, 2 * per, fold), 1) < per
    quarter = lax.rem(lax.broadcasted_iota(jnp.int32, (flat, 2 * hidden_units), 0), tall) // per

    def ffn(c):
        base = c * chunk

        def arrive(step):
            slot = base + step

            @pl.when(slot != me)
            def _():
                dispatch_copy(slot, slot).wait_recv()

        loop(chunk, arrive)
        block = disp[pl.ds(base, chunk)].reshape(flat, fold)
        total = jnp.zeros((flat, 2 * hidden_units), jnp.float32)
        for q in range(FOLD):
            part = jnp.dot(
                block, wgu_v[pl.ds(q * fold, fold), :], preferred_element_type=jnp.float32
            )
            total = jnp.where(quarter == q, part, total)
        total = total.reshape(chunk, 2, 2 * per, 2 * hidden_units)
        total = total[:, 0] + total[:, 1]
        total = (total + pltpu.roll(total, per, 1)).reshape(chunk * 2 * per, 2 * hidden_units)
        gate = total[:, :hidden_units]
        up = total[:, hidden_units:]
        activation = (gate / (1.0 + jnp.exp(-gate)) * up).astype(jnp.bfloat16)
        out = [
            jnp.dot(
                activation, wd_v[:, pl.ds(q * fold, fold)], preferred_element_type=jnp.float32
            ).reshape(chunk, 2 * per, fold)
            for q in range(FOLD)
        ]
        pout[pl.ds(base, chunk)] = jnp.concatenate(
            [jnp.where(low_row, out[0], out[1]), jnp.where(low_row, out[2], out[3])], axis=1
        ).astype(jnp.bfloat16)

        def give(step):
            other = base + step

            @pl.when((sec == 0) | (other != me))
            def _():
                return_copy(sec, me, other).start()

        loop(chunk, give)

    loop(n // chunk, ffn)

    @pl.when(sec == 0)
    def _():
        attend()
        back_copy().wait_recv()
        emit(xb_in[...])
        table_copy().wait_send()

    @pl.when(sec == 1)
    def _():
        ret[1, me] = pout[me]
        emit(combine(1, tab[...], True))
        back_copy().wait_send()

    def sent(step):
        dispatch_copy(me, lax.rem(me + step + 1, n)).wait_send()

    loop(n - 1, sent)

    def returned(step):
        @pl.when((sec == 0) | (step != me))
        def _():
            return_copy(sec, me, step).wait_send()

    loop(n, returned)
    pltpu.make_async_copy(ao_v, ao.at[0], out_sem).wait()


def shards(
    hidden_in,
    norm_gain,
    gate_weight,
    up_weight,
    down_weight,
    routes,
    route_weights,
    queries,
    latent_cache,
    lengths,
):
    n = lax.axis_size("expert")
    micro, rows, width = hidden_in.shape
    fold = width // FOLD
    tall = FOLD * micro * rows
    units = gate_weight.shape[2]
    heads = queries.shape[3]
    vmem = pl.BlockSpec(memory_space=pltpu.VMEM)
    smem = pl.BlockSpec(memory_space=pltpu.SMEM)
    far = pl.BlockSpec(memory_space=pl.ANY)
    dma = pltpu.SemaphoreType.DMA
    bf16, f32 = jnp.bfloat16, jnp.float32
    return pl.pallas_call(
        functools.partial(kernel, n),
        out_shape=(
            jax.ShapeDtypeStruct((1, micro, rows, width), bf16),
            jax.ShapeDtypeStruct((1, micro, rows, heads, LAT), bf16),
        ),
        in_specs=[vmem, vmem, far, far, far, vmem, vmem, far, far, smem],
        out_specs=(vmem, far),
        scratch_shapes=[
            pltpu.VMEM((tall, fold), f32),
            pltpu.VMEM((tall, fold), f32),
            pltpu.VMEM((tall, routes.shape[3]), jnp.int32),
            pltpu.VMEM((tall, routes.shape[3]), f32),
            pltpu.VMEM((tall, 128), f32),
            pltpu.VMEM((tall, 128), f32),
            pltpu.VMEM((tall, fold), bf16),
            pltpu.VMEM((n, tall, fold), bf16),
            pltpu.VMEM((n, tall, fold), bf16),
            pltpu.VMEM((2, n, tall, fold), bf16),
            pltpu.VMEM((tall, fold), bf16),
            pltpu.VMEM((tall, fold), bf16),
            pltpu.VMEM((width, 2 * units), bf16),
            pltpu.VMEM((units, width), bf16),
            pltpu.VMEM(queries.shape[1:], bf16),
            pltpu.VMEM(latent_cache.shape[1:], bf16),
            pltpu.VMEM((micro, rows, heads, LAT), bf16),
            dma((5,)),
            dma,
            dma((n,)),
            dma((n,)),
            dma((n,)),
            dma((2, n)),
            dma,
            dma,
            dma,
            dma,
        ],
        compiler_params=pltpu.CompilerParams(
            collective_id=0, has_side_effects=True, vmem_limit_bytes=56 * 1024 * 1024
        ),
    )(
        hidden_in,
        norm_gain,
        gate_weight,
        up_weight,
        down_weight,
        routes,
        route_weights,
        queries,
        latent_cache,
        lengths,
    )


def solution(mesh):
    return jax.shard_map(
        shards,
        mesh=mesh,
        in_specs=(
            P(None, ("groups", "expert"), None),
            P("section", None),
            P("section", None, "expert"),
            P("section", None, "expert"),
            P("section", "expert", None),
            P("section", None, ("groups", "expert"), None),
            P("section", None, ("groups", "expert"), None),
            P("section", None, ("groups", "expert"), None, None),
            P("section", None, ("groups", "expert"), None, None),
            P(None, ("groups", "expert")),
        ),
        out_specs=(
            P("section", None, ("groups", "expert"), None),
            P("section", None, ("groups", "expert"), None, None),
        ),
        check_vma=False,
    )
```

time: 87.8 us -> 31.8 us (0.36)
  the two profiles are of different devices: /device:TPU:0 before, /device:TPU:1 now
where the time goes in v1:
time: 31.8 us; the launch traced here: 31.6 us
  Pallas kernels  27.9 us (88%)
  local copies, waits for them, and re-layouts  3.05 us (10%)
  between operations  0.64 us (2%)
    pallas_call x1, Pallas kernels, shards(): pl.pallas_call(functools.partial(kernel, n), out_shape=(jax.ShapeDtypeStr...  27.9 us
    unnamed x2, local copies, waits for them, and re-layouts  3.05 us

profile of v1, /device:TPU:1, one launch (start us, length us, event | category | flops | bytes accessed | tf_op | source)
XLA Modules:
  0.0 31.6 jit_solution(208942384355815171)
XLA Ops:
  0.6 27.9 %shard_map.113 = (bf16[1,2,2,3584]{3,2,1,0:T(2,128)(2,1)}, bf16[1,2,2,64,512]{4,3,2,1,0:T(8,128)(2,1)}) custom-call(bf16[2,2,3584]{2,1,0:T(2,128)(2,1)} %hid.1, f32[1,3584]{1,0:T(1,128)} %gain.1, bf16[1,3584,128]{2,1,0:T(8,128)(2,1)} %wg.1, bf16[1,3584,128]{2,1,0:T(8,128)(2,1)} %wu.1, bf16[1,128,3584]{2,1,0:T(8,128)(2,1)} %wd.1, s32[1,2,2,4]{3,2,1,0:T(2,128)} %routes.1, ...), custom_call_target="tpu_custom_call" | custom-call | tf_op jit(solution)/shard_map/pallas_call | solution.py:354
  28.5 1.4 %copy.14 = bf16[1,2,2,3584]{3,2,1,0:T(2,128)(2,1)} copy(bf16[1,2,2,3584]{3,2,1,0:T(2,128)(2,1)} %get-tuple-element.4) | data formatting | bytes 57344
  29.9 1.7 %copy.15 = bf16[1,2,2,64,512]{4,3,2,1,0:T(8,128)(2,1)} copy(bf16[1,2,2,64,512]{4,3,2,1,0:T(8,128)(2,1)} %get-tuple-element.5) | data formatting | bytes 524288

commit v2 on v1

--- a/solution.py
+++ b/solution.py
@@ -27,18 +27,23 @@
 
 def kernel(
     n,
-    hid,
-    gain,
+    hid_far,
+    gain_far,
     wg,
     wu,
     wd,
+    routes_far,
+    rweights_far,
+    queries,
+    cache,
+    lens_far,
+    lo,
+    ao_v,
+    hid,
+    gain,
     routes,
     rweights,
-    queries,
-    cache,
     lens,
-    lo,
-    ao,
     xs,
     g16,
     rt16,
@@ -55,9 +60,7 @@
     wd_v,
     q_v,
     c_v,
-    ao_v,
     load_sem,
-    out_sem,
     d_send,
     d_recv,
     r_send,
@@ -76,6 +79,27 @@
     hidden_units = wg.shape[2]
     group = n // EXPERTS
 
+    barrier = pltpu.get_barrier_semaphore()
+
+    def apart(step):
+        return lax.rem(me + step + 1, n)
+
+    @pl.when(sec == 0)
+    def _():
+        def greet(step):
+            pl.semaphore_signal(
+                barrier,
+                inc=1,
+                device_id={"expert": apart(step)},
+                device_id_type=pl.DeviceIdType.MESH,
+            )
+
+        loop(n - 1, greet)
+
+    pl.semaphore_signal(
+        barrier, inc=1, device_id={"section": 1 - sec}, device_id_type=pl.DeviceIdType.MESH
+    )
+
     loads = [
         pltpu.make_async_copy(wg.at[0], wgu_v.at[:, pl.ds(0, hidden_units)], load_sem.at[0]),
         pltpu.make_async_copy(
@@ -84,29 +108,24 @@
         pltpu.make_async_copy(wd.at[0], wd_v, load_sem.at[2]),
         pltpu.make_async_copy(queries.at[0], q_v, load_sem.at[3]),
         pltpu.make_async_copy(cache.at[0], c_v, load_sem.at[4]),
+        pltpu.make_async_copy(lens_far, lens, load_sem.at[5]),
     ]
-    for copy in loads:
+    small = [
+        pltpu.make_async_copy(far, near, load_sem.at[6 + place])
+        for place, (far, near) in enumerate(
+            [
+                (hid_far, hid),
+                (gain_far, gain),
+                (routes_far, routes),
+                (rweights_far, rweights),
+            ]
+        )
+    ]
+    for copy in small + loads:
         copy.start()
 
-    barrier = pltpu.get_barrier_semaphore()
-
-    def greet(step):
-        other = lax.rem(me + step + 1, n)
-        pl.semaphore_signal(
-            barrier, inc=1, device_id={"expert": other}, device_id_type=pl.DeviceIdType.MESH
-        )
-
-    def greet_across(step):
-        other = lax.rem(me + step, n)
-        pl.semaphore_signal(
-            barrier,
-            inc=1,
-            device_id={"section": 1 - sec, "expert": other},
-            device_id_type=pl.DeviceIdType.MESH,
-        )
-
-    loop(n - 1, greet)
-    loop(n, greet_across)
+    for copy in small:
+        copy.wait()
 
     for q in range(FOLD):
         columns = pl.ds(q * fold, fold)
@@ -167,6 +186,7 @@
     def attend():
         loads[3].wait()
         loads[4].wait()
+        loads[5].wait()
         positions = lax.broadcasted_iota(jnp.int32, (queries.shape[3], cache.shape[3]), 1)
         for m in range(micro):
             for r in range(rows):
@@ -183,10 +203,9 @@
                 scores = jnp.where(positions < lens[m, r], scores, -jnp.inf)
                 expanded = jnp.exp(scores - jnp.max(scores, axis=1, keepdims=True))
                 probs = (expanded / jnp.sum(expanded, axis=1, keepdims=True)).astype(jnp.bfloat16)
-                ao_v[m, r] = jnp.dot(
+                ao_v[0, m, r] = jnp.dot(
                     probs, entries[:, :LAT], preferred_element_type=jnp.float32
                 ).astype(jnp.bfloat16)
-        pltpu.make_async_copy(ao_v, ao.at[0], out_sem).start()
 
     def combine(phase, weights, skip_own):
         total = xs[...]
@@ -219,35 +238,45 @@
                     pl.ds(q * per + m * rows, rows), :
                 ].astype(jnp.bfloat16)
 
-    pl.semaphore_wait(barrier, 2 * n - 1)
+    def normalise():
+        wide = xs[...]
+        squares = jnp.sum(wide * wide, axis=1, keepdims=True)
+        halves = jnp.broadcast_to(squares[: tall // 2] + squares[tall // 2 :], (tall // 2, 128))
+        halves = halves + pltpu.roll(halves, per, 0)
+        scale = lax.rsqrt(halves[:, :1] / width + 1e-06)
+        scale = jnp.concatenate([scale, scale], axis=0)
+        normed = (wide * scale * g16[...]).astype(jnp.bfloat16)
+        sbuf[...] = normed
+        disp[me] = normed
 
     @pl.when(sec == 0)
     def _():
-        table_copy().start()
+        normalise()
+        pl.semaphore_wait(barrier, n)
 
     @pl.when(sec == 1)
     def _():
+        pl.semaphore_wait(barrier, 1)
         attend()
         table_copy().wait_recv()
         first = combine(0, tab_in[...], False)
         xb[...] = first
+        xs[...] = first.astype(jnp.float32)
+        normalise()
+
+    def send(step):
+        dispatch_copy(me, apart(step)).start()
+
+    loop(n - 1, send)
+
+    @pl.when(sec == 0)
+    def _():
+        table_copy().start()
+
+    @pl.when(sec == 1)
+    def _():
         back_copy().start()
-        xs[...] = first.astype(jnp.float32)
-
-    wide = xs[...]
-    squares = jnp.sum(wide * wide, axis=1, keepdims=True)
-    halves = jnp.broadcast_to(squares[: tall // 2] + squares[tall // 2 :], (tall // 2, 128))
-    halves = halves + pltpu.roll(halves, per, 0)
-    scale = lax.rsqrt(halves[:, :1] / width + 1e-06)
-    scale = jnp.concatenate([scale, scale], axis=0)
-    normed = (wide * scale * g16[...]).astype(jnp.bfloat16)
-    sbuf[...] = normed
-    disp[me] = normed
-
-    def send(step):
-        dispatch_copy(me, lax.rem(me + step + 1, n)).start()
-
-    loop(n - 1, send)
+
     for copy in loads[:3]:
         copy.wait()
 
@@ -290,14 +319,24 @@
             [jnp.where(low_row, out[0], out[1]), jnp.where(low_row, out[2], out[3])], axis=1
         ).astype(jnp.bfloat16)
 
-        def give(step):
-            other = base + step
-
-            @pl.when((sec == 0) | (other != me))
+        if n == chunk:
+            for step in range(n - 1):
+                return_copy(sec, me, apart(step)).start()
+
+            @pl.when(sec == 0)
             def _():
-                return_copy(sec, me, other).start()
-
-        loop(chunk, give)
+                return_copy(sec, me, me).start()
+
+        else:
+
+            def give(step):
+                other = base + step
+
+                @pl.when((sec == 0) | (other != me))
+                def _():
+                    return_copy(sec, me, other).start()
+
+            loop(chunk, give)
 
     loop(n // chunk, ffn)
 
@@ -325,7 +364,6 @@
             return_copy(sec, me, step).wait_send()
 
     loop(n, returned)
-    pltpu.make_async_copy(ao_v, ao.at[0], out_sem).wait()
 
 
 def shards(
@@ -347,19 +385,23 @@
     units = gate_weight.shape[2]
     heads = queries.shape[3]
     vmem = pl.BlockSpec(memory_space=pltpu.VMEM)
-    smem = pl.BlockSpec(memory_space=pltpu.SMEM)
-    far = pl.BlockSpec(memory_space=pl.ANY)
+    far = pl.BlockSpec(memory_space=pltpu.HBM)
     dma = pltpu.SemaphoreType.DMA
     bf16, f32 = jnp.bfloat16, jnp.float32
     return pl.pallas_call(
         functools.partial(kernel, n),
         out_shape=(
-            jax.ShapeDtypeStruct((1, micro, rows, width), bf16),
-            jax.ShapeDtypeStruct((1, micro, rows, heads, LAT), bf16),
+            pltpu.VMEM((1, micro, rows, width), bf16),
+            pltpu.VMEM((1, micro, rows, heads, LAT), bf16),
         ),
-        in_specs=[vmem, vmem, far, far, far, vmem, vmem, far, far, smem],
-        out_specs=(vmem, far),
+        in_specs=[far] * 10,
+        out_specs=(vmem, vmem),
         scratch_shapes=[
+            pltpu.VMEM(hidden_in.shape, bf16),
+            pltpu.VMEM(norm_gain.shape, f32),
+            pltpu.VMEM(routes.shape, jnp.int32),
+            pltpu.VMEM(route_weights.shape, f32),
+            pltpu.SMEM(lengths.shape, jnp.int32),
             pltpu.VMEM((tall, fold), f32),
             pltpu.VMEM((tall, fold), f32),
             pltpu.VMEM((tall, routes.shape[3]), jnp.int32),
@@ -376,9 +418,7 @@
             pltpu.VMEM((units, width), bf16),
             pltpu.VMEM(queries.shape[1:], bf16),
             pltpu.VMEM(latent_cache.shape[1:], bf16),
-            pltpu.VMEM((micro, rows, heads, LAT), bf16),
-            dma((5,)),
-            dma,
+            dma((10,)),
             dma((n,)),
             dma((n,)),
             dma((n,)),

time: 31.8 us -> 28.4 us (0.89)
  local copies, waits for them, and re-layouts: 3.05 us -> 1.31 us
  Pallas kernels: 27.9 us -> 26.3 us
    unnamed x2, local copies, waits for them, and re-layouts: 3.05 us -> 1.31 us
    pallas_call x1, Pallas kernels: 27.9 us -> 26.3 us  [shards(): pl.pallas_call(functools.partial(kernel, n), out_shape=(pltpu.VMEM((1, mi...]
where the time goes in v2:
time: 28.4 us; the launch traced here: 28.2 us
  Pallas kernels  26.3 us (93%)
  local copies, waits for them, and re-layouts  1.31 us (5%)
  between operations  0.64 us (2%)
    pallas_call x1, Pallas kernels, shards(): pl.pallas_call(functools.partial(kernel, n), out_shape=(pltpu.VMEM((1, mi...  26.3 us
    unnamed x2, local copies, waits for them, and re-layouts  1.31 us

profile of v2, /device:TPU:1, one launch (start us, length us, event | category | flops | bytes accessed | tf_op | source)
XLA Modules:
  0.0 28.2 jit_solution(6818102658833260184)
XLA Ops:
  0.6 26.3 %shard_map.113 = (bf16[1,2,2,3584]{3,2,1,0:T(2,128)(2,1)S(1)}, bf16[1,2,2,64,512]{4,3,2,1,0:T(8,128)(2,1)S(1)}) custom-call(bf16[2,2,3584]{2,1,0:T(2,128)(2,1)} %hid_far.1, f32[1,3584]{1,0:T(1,128)} %gain_far.1, bf16[1,3584,128]{2,1,0:T(8,128)(2,1)} %wg.1, bf16[1,3584,128]{2,1,0:T(8,128)(2,1)} %wu.1, bf16[1,128,3584]{2,1,0:T(8,128)(2,1)} %wd.1, ...), custom_call_target="tpu_custom_call" | custom-call | tf_op jit(solution)/shard_map/pallas_call | solution.py:391
  26.9 0.6 %copy.14 = bf16[1,2,2,3584]{3,2,1,0:T(2,128)(2,1)} copy(bf16[1,2,2,3584]{3,2,1,0:T(2,128)(2,1)S(1)} %get-tuple-element.2) | data formatting | bytes 57344
  27.5 0.7 %copy.15 = bf16[1,2,2,64,512]{4,3,2,1,0:T(8,128)(2,1)} copy(bf16[1,2,2,64,512]{4,3,2,1,0:T(8,128)(2,1)S(1)} %get-tuple-element.3) | data formatting | bytes 524288

commit v3 on v2

--- a/solution.py
+++ b/solution.py
@@ -366,6 +366,17 @@
     loop(n, returned)
 
 
+def hand_out(layer, attention, layer_to, attention_to, sems):
+    copies = [
+        pltpu.make_async_copy(attention, attention_to, sems.at[0]),
+        pltpu.make_async_copy(layer, layer_to, sems.at[1]),
+    ]
+    for copy in copies:
+        copy.start()
+    for copy in copies:
+        copy.wait()
+
+
 def shards(
     hidden_in,
     norm_gain,
@@ -388,7 +399,7 @@
     far = pl.BlockSpec(memory_space=pltpu.HBM)
     dma = pltpu.SemaphoreType.DMA
     bf16, f32 = jnp.bfloat16, jnp.float32
-    return pl.pallas_call(
+    results = pl.pallas_call(
         functools.partial(kernel, n),
         out_shape=(
             pltpu.VMEM((1, micro, rows, width), bf16),
@@ -443,6 +454,13 @@
         latent_cache,
         lengths,
     )
+    return pl.pallas_call(
+        hand_out,
+        out_shape=tuple(jax.ShapeDtypeStruct(value.shape, value.dtype) for value in results),
+        in_specs=[vmem] * 2,
+        out_specs=(far, far),
+        scratch_shapes=[dma((2,))],
+    )(*[pltpu.with_memory_space_constraint(value, pltpu.VMEM) for value in results])
 
 
 def solution(mesh):

time: 28.4 us -> 27.8 us (0.979)
  local copies, waits for them, and re-layouts: 1.31 us -> 0 us
  Pallas kernels: 26.3 us -> 27 us
    unnamed x2 -> x0, local copies, waits for them, and re-layouts: 1.31 us -> none
    pallas_call x0 -> x1, Pallas kernels: none -> 0.72 us  [shards(): pl.pallas_call(hand_out, out_shape=tuple((jax.ShapeDtypeStruct(value.shap...]
where the time goes in v3:
time: 27.8 us; the launch traced here: 27.6 us
  Pallas kernels  27 us (97%)
  between operations  0.64 us (2%)
    pallas_call x1, Pallas kernels, shards(): pl.pallas_call(functools.partial(kernel, n), out_shape=(pltpu.VMEM((1, mi...  26.3 us
    pallas_call x1, Pallas kernels, shards(): pl.pallas_call(hand_out, out_shape=tuple((jax.ShapeDtypeStruct(value.shap...  0.72 us

profile of v3, /device:TPU:1, one launch (start us, length us, event | category | flops | bytes accessed | tf_op | source)
XLA Modules:
  0.0 27.6 jit_solution(5062212318720174946)
XLA Ops:
  0.6 26.3 %shard_map.113 = (bf16[1,2,2,3584]{3,2,1,0:T(2,128)(2,1)S(1)}, bf16[1,2,2,64,512]{4,3,2,1,0:T(8,128)(2,1)S(1)}) custom-call(bf16[2,2,3584]{2,1,0:T(2,128)(2,1)} %hid_far.1, f32[1,3584]{1,0:T(1,128)} %gain_far.1, bf16[1,3584,128]{2,1,0:T(8,128)(2,1)} %wg.1, bf16[1,3584,128]{2,1,0:T(8,128)(2,1)} %wu.1, bf16[1,128,3584]{2,1,0:T(8,128)(2,1)} %wd.1, ...), custom_call_target="tpu_custom_call" | custom-call | tf_op jit(solution)/shard_map/pallas_call | solution.py:402
  26.9 0.7 %shard_map.114 = (bf16[1,2,2,3584]{3,2,1,0:T(2,128)(2,1)}, bf16[1,2,2,64,512]{4,3,2,1,0:T(8,128)(2,1)}) custom-call(bf16[1,2,2,3584]{3,2,1,0:T(2,128)(2,1)S(1)} %get-tuple-element.4.layer, bf16[1,2,2,64,512]{4,3,2,1,0:T(8,128)(2,1)S(1)} %get-tuple-element.5.attention), custom_call_target="tpu_custom_call" | custom-call | tf_op jit(solution)/shard_map/pallas_call | solution.py:457
